TPU v7x, 32 devices: a whole 2x2x4 slice. The times are simulated.
32 devices in a mesh: dp: 4 (over y, x), fsdp: 8 (over z, core).
Axes of the slice: x: 2, y: 2, z: 4, core: 2. Of those that a mesh axis runs over, the one named last changes fastest.
Arguments:
- history: float32 [65536, 3600], P(('dp', 'fsdp')), may hold values from -6 to 6
- later_observed: float32 [65536, 720], P(('dp', 'fsdp')), may hold values from -6 to 6
- lengths: int32 [65536], P(('dp', 'fsdp')), may hold values from 900 to 3600
- counted_flags: int32 [65536, 720], P(('dp', 'fsdp')), may hold values from 0 to 1
- series: int32 [65536], P(('dp', 'fsdp')), may hold values from 0 to 1022
- coarse_in: float32 [450, 512], P(None, 'fsdp'), may hold values from -0.25 to 0.25
- middle: float32 [4, 512, 512], P(None, None, 'fsdp'), may hold values from -0.25 to 0.25
- rough_final_matrix: float32 [512, 180], P('fsdp'), may hold values from -0.25 to 0.25
- fine_in: float32 [3600, 512], P(None, 'fsdp'), may hold values from -0.09375 to 0.09375
- sharp_final_matrix: float32 [512, 720], P('fsdp'), may hold values from -0.25 to 0.25
- offset_vectors: float32 [3972], replicated, may hold values from -0.3 to 0.3
- coarse_in_mean: float32 [450, 512], P(None, 'fsdp'), may hold values from -8.712071e-08 to 8.712071e-08
- middle_mean: float32 [4, 512, 512], P(None, None, 'fsdp'), may hold values from -1.7424142e-06 to 1.7424142e-06
- rough_final_first: float32 [512, 180], P('fsdp'), may hold values from -1.7424142e-06 to 1.7424142e-06
- fine_in_mean: float32 [3600, 512], P(None, 'fsdp'), may hold values from -1.7424142e-06 to 1.7424142e-06
- sharp_final_first: float32 [512, 720], P('fsdp'), may hold values from -1.7424142e-06 to 1.7424142e-06
- biases_mean: float32 [3972], replicated, may hold values from -5.280043e-06 to 5.280043e-06
- coarse_in_square: float32 [450, 512], P(None, 'fsdp'), may hold values from 6.969713e-17 to 2.7878853e-16
- middle_square: float32 [4, 512, 512], P(None, None, 'fsdp'), may hold values from 2.7878854e-14 to 1.1151542e-13
- rough_final_second: float32 [512, 180], P('fsdp'), may hold values from 2.7878854e-14 to 1.1151542e-13
- fine_in_square: float32 [3600, 512], P(None, 'fsdp'), may hold values from 2.7878854e-14 to 1.1151542e-13
- sharp_final_second: float32 [512, 720], P('fsdp'), may hold values from 2.7878854e-14 to 1.1151542e-13
- biases_square: float32 [3972], replicated, may hold values from 2.7878855e-13 to 1.1151542e-12
Outputs:
- loss_sum: float32 [], replicated
- usable_tally: float32 [], replicated
- grad_norm: float32 [], replicated
- new_coarse_in: float32 [450, 512], P(None, 'fsdp')
- new_middle: float32 [4, 512, 512], P(None, None, 'fsdp')
- new_coarse_out: float32 [512, 180], P('fsdp')
- new_fine_in: float32 [3600, 512], P(None, 'fsdp')
- new_fine_out: float32 [512, 720], P('fsdp')
- new_biases: float32 [3972], replicated
- new_coarse_in_mean: float32 [450, 512], P(None, 'fsdp')
- new_middle_mean: float32 [4, 512, 512], P(None, None, 'fsdp')
- new_coarse_out_mean: float32 [512, 180], P('fsdp')
- new_fine_in_mean: float32 [3600, 512], P(None, 'fsdp')
- new_fine_out_mean: float32 [512, 720], P('fsdp')
- new_biases_mean: float32 [3972], replicated
- new_coarse_in_square: float32 [450, 512], P(None, 'fsdp')
- new_middle_square: float32 [4, 512, 512], P(None, None, 'fsdp')
- new_coarse_out_square: float32 [512, 180], P('fsdp')
- new_fine_in_square: float32 [3600, 512], P(None, 'fsdp')
- new_fine_out_square: float32 [512, 720], P('fsdp')
- new_biases_square: float32 [3972], replicated
All inputs are finite; a program needn't handle non-finite values.
Results may differ from a plain program's by a relative error of at most 0.0045.
Values may be sent and summed in bfloat16 or wider, within the bound.
No kernel may reach another device: no remote copies, remote signals or barrier semaphores. Data moves between devices by JAX's collectives and lax.ppermute only.
A program may use at most 256 MiB of HBM per device.

v0:
```python
import jax
import jax.numpy as jnp
from jax import lax
from jax.sharding import PartitionSpec as P

LOOKBACK = 3600
INNER_WIDTH = 512
POOL = 8
RATIO = 24
SERIES = 1024
STEP = 10
LP = 450
HINDSIGHT_WTS = 150
OUTLOOK_WTS = 30


exact_matmul_mode = lax.Precision.HIGHEST
beta_first = 0.9
beta_second = 0.999
learn_rate = 0.01
weight_decay = 0.01
adam_epsilon = 1e-08
clip_level = 0.01


def lerp_weights():
    offsets = jnp.arange(RATIO, dtype=jnp.float32)
    middle_at = RATIO // 2
    early = offsets < middle_at
    ahead = (offsets + 0.5 + middle_at) / RATIO
    behind = (offsets + 0.5 - middle_at) / RATIO
    weight_prev = jnp.where(early, 1.0 - ahead, 0.0)
    weight_same = jnp.where(early, ahead, 1.0 - behind)
    weight_next = jnp.where(early, 0.0, behind)
    return (weight_prev, weight_same, weight_next)


def linear_upsample(coeffs):
    rows_here, count = coeffs.shape
    weight_prev, weight_same, weight_next = lerp_weights()
    previous = jnp.concatenate([coeffs[:, :1], coeffs[:, :-1]], 1)
    following = jnp.concatenate([coeffs[:, 1:], coeffs[:, -1:]], 1)
    spread_out = (
        previous[:, :, None] * weight_prev
        + coeffs[:, :, None] * weight_same
        + following[:, :, None] * weight_next
    )
    return spread_out.reshape(rows_here, count * RATIO)


def lerp_back(grad):
    rows_here = grad.shape[0]
    count = grad.shape[1] // RATIO
    weight_prev, weight_same, weight_next = lerp_weights()
    parts = grad.reshape(rows_here, count, RATIO)
    to_prev = jnp.sum(parts * weight_prev, 2)
    to_same = jnp.sum(parts * weight_same, 2)
    to_next = jnp.sum(parts * weight_next, 2)
    nothing = jnp.zeros((rows_here, 1), jnp.float32)
    from_prev = jnp.concatenate([to_prev[:, 0:1] + to_prev[:, 1:2], to_prev[:, 2:], nothing], 1)
    from_next = jnp.concatenate([nothing, to_next[:, :-2], to_next[:, -2:-1] + to_next[:, -1:]], 1)
    return to_same + from_prev + from_next


def split_offsets(offset_vectors):
    hidden_bias = offset_vectors[: 6 * INNER_WIDTH].reshape(6, INNER_WIDTH)
    rough_final_part = offset_vectors[
        6 * INNER_WIDTH : 6 * INNER_WIDTH + HINDSIGHT_WTS + OUTLOOK_WTS
    ]
    sharp_final_part = offset_vectors[6 * INNER_WIDTH + HINDSIGHT_WTS + OUTLOOK_WTS :]
    return (
        (hidden_bias[0], hidden_bias[1], hidden_bias[2], rough_final_part),
        (hidden_bias[3], hidden_bias[4], hidden_bias[5], sharp_final_part),
    )


def silu_slope(pre):
    sigmoid_v = jax.nn.sigmoid(pre)
    return sigmoid_v * (1.0 + pre * (1.0 - sigmoid_v))


def run_block(entering, mats, offsets):
    stored = []
    current = entering
    for layer_at in range(4):
        lowered = current.astype(jnp.bfloat16)
        pre = (
            jnp.dot(lowered, mats[layer_at], preferred_element_type=jnp.float32) + offsets[layer_at]
        )
        stored.append((lowered, pre))
        current = jax.nn.silu(pre) if layer_at < 3 else pre
    return (current, stored)


def back_block(stored, mats, upstream, need_input):
    weight_grads = [None, None, None, None]
    bias_grads = [None, None, None, None]
    for layer_at in (3, 2, 1, 0):
        lowered, pre = stored[layer_at]
        if layer_at < 3:
            upstream = upstream * silu_slope(pre)
        rounded = upstream.astype(jnp.bfloat16)
        weight_grads[layer_at] = lax.dot_general(
            lowered, rounded, (((0,), (0,)), ((), ())), preferred_element_type=jnp.float32
        )
        bias_grads[layer_at] = jnp.sum(rounded.astype(jnp.float32), axis=0)
        if layer_at > 0 or need_input:
            upstream = lax.dot_general(
                rounded,
                mats[layer_at],
                (((1,), (1,)), ((), ())),
                preferred_element_type=jnp.float32,
            )
    return (weight_grads, bias_grads, upstream)


def adam_step(weight, mean_old, square_old, grad, factor):
    clipped = grad * factor
    mean_new = beta_first * mean_old + (1.0 - beta_first) * clipped
    square_new = beta_second * square_old + (1.0 - beta_second) * clipped * clipped
    mean_hat = mean_new / (1.0 - beta_first**STEP)
    square_hat = square_new / (1.0 - beta_second**STEP)
    weight_new = weight - learn_rate * (
        mean_hat / (jnp.sqrt(square_hat) + adam_epsilon) + weight_decay * weight
    )
    return (weight_new, mean_new, square_new)


def body(
    history,
    later_observed,
    lengths,
    counted_flags,
    series,
    coarse_in,
    middle,
    rough_final_matrix,
    fine_in,
    sharp_final_matrix,
    offset_vectors,
    coarse_in_mean,
    middle_mean,
    rough_final_first,
    fine_in_mean,
    sharp_final_first,
    biases_mean,
    coarse_in_square,
    middle_square,
    rough_final_second,
    fine_in_square,
    sharp_final_second,
    biases_square,
):
    rows_here = history.shape[0]
    steps_iota = lax.broadcasted_iota(jnp.int32, history.shape, 1)
    observed_history = (steps_iota >= LOOKBACK - lengths[:, None]).astype(jnp.float32)
    masked = history * observed_history
    row_terms = jnp.stack(
        [jnp.sum(masked, 1), jnp.sum(masked * history, 1), jnp.sum(observed_history, 1)], 1
    )
    one_hot = (series[:, None] == lax.broadcasted_iota(jnp.int32, (1, SERIES), 1)).astype(
        jnp.float32
    )
    local_table = jnp.einsum("ws,wk->sk", one_hot, row_terms, precision=exact_matmul_mode)
    outlook_extent = counted_flags.astype(jnp.float32)
    device_tally = jnp.sum(outlook_extent)
    table = lax.psum(local_table, ("dp", "fsdp"))
    counted = jnp.maximum(table[:, 2], 1.0)
    centre = table[:, 0] / counted
    spread = jnp.sqrt(table[:, 1] / counted + 1e-05)
    looked = jnp.dot(one_hot, jnp.stack([centre, spread], 1), precision=exact_matmul_mode)
    rescaled_input = (history - looked[:, 0:1]) / looked[:, 1:2] * observed_history
    goal_entries = (later_observed - looked[:, 0:1]) / looked[:, 1:2]
    gathered = (
        lax.all_gather(coarse_in.astype(jnp.bfloat16), "fsdp", axis=1, tiled=True),
        lax.all_gather(middle.astype(jnp.bfloat16), "fsdp", axis=2, tiled=True),
        lax.all_gather(rough_final_matrix.astype(jnp.bfloat16), "fsdp", axis=0, tiled=True),
        lax.all_gather(fine_in.astype(jnp.bfloat16), "fsdp", axis=1, tiled=True),
        lax.all_gather(sharp_final_matrix.astype(jnp.bfloat16), "fsdp", axis=0, tiled=True),
    )
    coarse_mats = (gathered[0], gathered[1][0], gathered[1][1], gathered[2])
    fine_mats = (gathered[3], gathered[1][2], gathered[1][3], gathered[4])
    coarse_offsets, fine_offsets = split_offsets(offset_vectors)
    pooled = jnp.mean(rescaled_input.reshape(rows_here, LP, POOL), axis=2)
    knot_weights, coarse_stored = run_block(pooled, coarse_mats, coarse_offsets)
    backcast = linear_upsample(knot_weights[:, :HINDSIGHT_WTS])
    residue = (rescaled_input - backcast) * observed_history
    refined_entry, fine_stored = run_block(residue, fine_mats, fine_offsets)
    estimate_output = linear_upsample(knot_weights[:, HINDSIGHT_WTS:]) + refined_entry
    misfit_amount = (estimate_output - goal_entries) * outlook_extent
    local_loss = jnp.sum(misfit_amount * misfit_amount)
    usable_tally = lax.psum(device_tally, ("dp", "fsdp"))
    outlook_derivative = 2.0 * misfit_amount * outlook_extent / usable_tally
    fine_wg, fine_bg, residue_grad = back_block(fine_stored, fine_mats, outlook_derivative, True)
    back_grad = lerp_back(-residue_grad * observed_history)
    fore_coef_grad = lerp_back(outlook_derivative)
    coarse_wg, coarse_bg, leftover = back_block(
        coarse_stored, coarse_mats, jnp.concatenate([back_grad, fore_coef_grad], 1), False
    )
    middle_grad = jnp.stack([coarse_wg[1], coarse_wg[2], fine_wg[1], fine_wg[2]])
    grads = (coarse_wg[0], middle_grad, coarse_wg[3], fine_wg[0], fine_wg[3])
    partial_grads = (
        lax.psum_scatter(grads[0], "fsdp", scatter_dimension=1, tiled=True),
        lax.psum_scatter(grads[1], "fsdp", scatter_dimension=2, tiled=True),
        lax.psum_scatter(grads[2], "fsdp", scatter_dimension=0, tiled=True),
        lax.psum_scatter(grads[3], "fsdp", scatter_dimension=1, tiled=True),
        lax.psum_scatter(grads[4], "fsdp", scatter_dimension=0, tiled=True),
    )
    shards = lax.psum(
        (partial_grads[0], partial_grads[1], partial_grads[2], partial_grads[3], partial_grads[4]),
        "dp",
    )
    bias_local = jnp.concatenate(
        [
            coarse_bg[0],
            coarse_bg[1],
            coarse_bg[2],
            fine_bg[0],
            fine_bg[1],
            fine_bg[2],
            coarse_bg[3],
            fine_bg[3],
        ]
    )
    bias_grad, loss_sum = lax.psum((bias_local, local_loss), ("dp", "fsdp"))
    square_part = jnp.zeros((), jnp.float32)
    for fragment in shards:
        square_part = square_part + jnp.sum(fragment * fragment)
    total_square = lax.psum(square_part, "fsdp") + jnp.sum(bias_grad * bias_grad)
    grad_norm = jnp.sqrt(total_square)
    factor = clip_level / jnp.maximum(grad_norm, clip_level)
    params = (coarse_in, middle, rough_final_matrix, fine_in, sharp_final_matrix, offset_vectors)
    all_grads = (shards[0], shards[1], shards[2], shards[3], shards[4], bias_grad)
    means = (
        coarse_in_mean,
        middle_mean,
        rough_final_first,
        fine_in_mean,
        sharp_final_first,
        biases_mean,
    )
    squares = (
        coarse_in_square,
        middle_square,
        rough_final_second,
        fine_in_square,
        sharp_final_second,
        biases_square,
    )
    results = [
        adam_step(params[item], means[item], squares[item], all_grads[item], factor)
        for item in range(6)
    ]
    return (
        loss_sum,
        usable_tally,
        grad_norm,
        results[0][0],
        results[1][0],
        results[2][0],
        results[3][0],
        results[4][0],
        results[5][0],
        results[0][1],
        results[1][1],
        results[2][1],
        results[3][1],
        results[4][1],
        results[5][1],
        results[0][2],
        results[1][2],
        results[2][2],
        results[3][2],
        results[4][2],
        results[5][2],
    )


def solution(mesh):
    in_specs = (
        P(("dp", "fsdp"), None),
        P(("dp", "fsdp"), None),
        P(("dp", "fsdp")),
        P(("dp", "fsdp"), None),
        P(("dp", "fsdp")),
        P(None, "fsdp"),
        P(None, None, "fsdp"),
        P("fsdp", None),
        P(None, "fsdp"),
        P("fsdp", None),
        P(),
        P(None, "fsdp"),
        P(None, None, "fsdp"),
        P("fsdp", None),
        P(None, "fsdp"),
        P("fsdp", None),
        P(),
        P(None, "fsdp"),
        P(None, None, "fsdp"),
        P("fsdp", None),
        P(None, "fsdp"),
        P("fsdp", None),
        P(),
    )
    out_specs = (
        P(),
        P(),
        P(),
        P(None, "fsdp"),
        P(None, None, "fsdp"),
        P("fsdp", None),
        P(None, "fsdp"),
        P("fsdp", None),
        P(),
        P(None, "fsdp"),
        P(None, None, "fsdp"),
        P("fsdp", None),
        P(None, "fsdp"),
        P("fsdp", None),
        P(),
        P(None, "fsdp"),
        P(None, None, "fsdp"),
        P("fsdp", None),
        P(None, "fsdp"),
        P("fsdp", None),
        P(),
    )
    return jax.shard_map(body, mesh=mesh, in_specs=in_specs, out_specs=out_specs, check_vma=False)
```

profile of v0, /device:TPU:0, one launch (start us, length us, event | category | flops | bytes accessed | tf_op | source)
XLA Modules:
  0.0 693.7 jit_solution(873710399315005754)
XLA Ops:
  16.0 14.0 %select_reduce_fusion = (f32[2048]{0:T(1024)S(1)}, f32[2048]{0:T(1024)S(1)}, f32[2048]{0:T(1024)S(1)}) fusion(f32[2048,3600]{0,1:T(8,128)} %param.23, s32[2048]{0:T(1024)S(1)} %broadcast_subtract_fusion), kind=kLoop, calls=%fused_computation.1 | loop fusion | flops 51603456 | bytes 29523968 | tf_op jit(solution)/shard_map/reduce_sum | solution.py:159
  32.7 43.8 %all-reduce.2 = (f32[1024,3]{0,1:T(4,128)S(1)}, f32[]{:T(128)}) all-reduce(f32[1024,3]{0,1:T(4,128)S(1)} %fusion.7, f32[]{:T(128)} %convert_reduce_fusion.2), channel_id=1, replica_groups=mesh['dp'=4,'fsdp'=8] {'dp','fsdp'}, use_global_device_ids=true, to_apply=%region_3.0 | all-reduce | flops 3073 | bytes 24584 | tf_op jit(solution)/shard_map/psum | solution.py:167
  80.6 17.8 %bitcast_reduce_fusion = f32[2048,450]{0,1:T(8,128)} fusion(f32[2048]{0:T(1024)S(1)} %bitcast.119, f32[2048,3600]{0,1:T(8,128)} %param.23, f32[2048]{0:T(1024)S(1)} %bitcast.116, s32[2048]{0:T(1024)S(1)} %broadcast_subtract_fusion), kind=kLoop, calls=%fused_computation.11 | loop fusion | flops 35942400 | bytes 33202176 | tf_op jit(solution)/shard_map/reduce_sum | solution.py:184
  103.4 14.9 %all_gather.17 = bf16[512,180]{1,0:T(8,128)(2,1)S(1)} all-gather(bf16[64,180]{1,0:T(8,128)(2,1)S(1)} %convert_element_type.99), channel_id=1, replica_groups=mesh['dp'=4,'fsdp'=8] {'fsdp'}, dimensions={0}, use_global_device_ids=true | all-gather | bytes 207360 | tf_op jit(solution)/shard_map/all_gather | solution.py:177
  118.3 14.7 %all_gather.15 = bf16[450,512]{0,1:T(8,128)(2,1)S(1)} all-gather(bf16[450,64]{0,1:T(8,128)(2,1)S(1)} %convert_element_type.94), channel_id=1, replica_groups=mesh['dp'=4,'fsdp'=8] {'fsdp'}, dimensions={1}, use_global_device_ids=true | all-gather | bytes 518400 | tf_op jit(solution)/shard_map/all_gather | solution.py:175
  133.6 16.1 %all_gather.19 = bf16[512,720]{1,0:T(8,128)(2,1)S(1)} all-gather(bf16[64,720]{1,0:T(8,128)(2,1)S(1)} %convert_element_type.105), channel_id=1, replica_groups=mesh['dp'=4,'fsdp'=8] {'fsdp'}, dimensions={0}, use_global_device_ids=true | all-gather | bytes 829440 | tf_op jit(solution)/shard_map/all_gather | solution.py:179
  149.7 5.4 fusion.19
  158.9 5.1 multiply_convert_fusion.9
  168.3 21.8 %fusion.4 = bf16[2048,3600]{0,1:T(8,128)(2,1)} fusion(f32[3600]{0:T(1024)} %mul.562, f32[2048,150]{0,1:T(8,128)} %get-tuple-element.155, f32[3600]{0:T(1024)} %mul.556, f32[2048,150]{0,1:T(8,128)S(1)} %slice.193, f32[3600]{0:T(1024)} %mul.550, f32[2048,150]{0,1:T(8,128)} %get-tuple-element.154, s32[2048]{0:T(1024)S(1)} %broadcast_subtract_fusion, ...), kind=kLoop, calls=%fused_computation.7 | loop fusion | flops 88473600 | bytes 47990976 | tf_op jit(solution)/shard_map/convert_element_type | solution.py:86
  191.0 13.3 %fusion.64 = f32[2048,512]{1,0:T(8,128)S(1)} fusion(bf16[2048,3600]{0,1:T(8,128)(2,1)} %fusion.4, bf16[3600,512]{0,1:T(8,128)(2,1)} %all-gather.5.cloned.1.call-done), kind=kOutput, calls=%fused_computation.162 | convolution fusion | flops 7549747200 | bytes 22626304 | tf_op jit(solution)/shard_map/dot_general | solution.py:88
  236.4 15.4 %negate_select_fusion = f32[2048,3600]{0,1:T(8,128)} fusion(bf16[2048,512]{1,0:T(8,128)(2,1)} %get-tuple-element.149, bf16[3600,512]{0,1:T(8,128)(2,1)S(1)} %copy-done.48, s32[2048]{0:T(1024)S(1)} %broadcast_subtract_fusion), kind=kOutput, calls=%fused_computation.15 | convolution fusion | flops 7571865600 | bytes 35282944 | tf_op jit(solution)/shard_map/dot_general | solution.py:108
  251.8 23.3 %multiply_reduce_fusion = (f32[2048,150]{0,1:T(8,128)S(1)}, f32[2048,150]{0,1:T(8,128)S(1)}, f32[2048,150]{0,1:T(8,128)S(1)}) fusion(f32[2048,150,24]{0,2,1:T(8,128)} %bitcast.110, f32[24]{0:T(128)S(1)} %copy-done.34, f32[24]{0:T(128)S(1)} %copy-done.38, f32[24]{0:T(128)S(1)} %copy-done.36), kind=kLoop, calls=%fused_computation.12 | loop fusion | flops 43315200 | bytes 33177888 | tf_op jit(solution)/shard_map/reduce_sum | solution.py:58
  288.4 5.4 copy.66
  294.1 5.5 convert_reduce_fusion.8
  302.0 7.9 %fusion.48 = f32[512,720]{1,0:T(8,128)} fusion(f32[2048,720]{0,1:T(8,128)} %copy-done.1, f32[2048,512]{1,0:T(8,128)} %copy-done.3, f32[512]{0:T(512)S(1)} %copy-done.31), kind=kOutput, calls=%fused_computation.152 | convolution fusion | flops 1517715456 | bytes 11569152 | tf_op jit(solution)/shard_map/dot_general | solution.py:103
  309.9 14.9 %fusion.65 = f32[3600,512]{0,1:T(8,128)} fusion(bf16[2048,3600]{0,1:T(8,128)(2,1)} %fusion.4, bf16[2048,512]{1,0:T(8,128)(2,1)} %get-tuple-element.149), kind=kOutput, calls=%fused_computation.163 | convolution fusion | flops 7549747200 | bytes 24215552 | tf_op jit(solution)/shard_map/dot_general | solution.py:103
  329.4 60.5 %all-reduce.7.cloned.1.call-done = f32[4,512,512]{1,0,2:T(4,128)} async-done(((f32[4,512,512]{1,0,2:T(4,128)}), f32[4,512,512]{1,0,2:T(4,128)}) %all-reduce.7.cloned.1.call-update) | async-done | bytes 4194320
  392.0 32.5 %reduce-scatter.5.cloned.1.call-done = f32[450,64]{0,1:T(8,128)} async-done(((f32[450,512]{0,1:T(8,128)}), f32[450,64]{0,1:T(8,128)}) %reduce-scatter.5.cloned.1.call-update) | async-done | bytes 115216 | tf_op jit(solution)/shard_map/reduce_scatter | solution.py:203
  424.5 34.7 %reduce-scatter.11.cloned.1.call-done = f32[64,720]{1,0:T(8,128)} async-done(((f32[512,720]{1,0:T(8,128)}), f32[64,720]{1,0:T(8,128)}) %reduce-scatter.11.cloned.1.call-update) | async-done | bytes 184336 | tf_op jit(solution)/shard_map/reduce_scatter | solution.py:207
  459.2 82.2 %reduce-scatter.9.cloned.1.call-done = f32[3600,64]{0,1:T(8,128)} async-done(((f32[3600,512]{0,1:T(8,128)}), f32[3600,64]{0,1:T(8,128)}) %reduce-scatter.9.cloned.1.call-update) | async-done | bytes 921616 | tf_op jit(solution)/shard_map/reduce_scatter | solution.py:206
  541.7 38.5 %all-reduce.1 = (f32[]{:T(128)}, f32[3972]{0:T(1024)}) all-reduce(f32[]{:T(128)} %get-tuple-element.121, f32[3972]{0:T(1024)S(1)} %concatenate.40), channel_id=1, replica_groups=mesh['dp'=4,'fsdp'=8] {'dp','fsdp'}, use_global_device_ids=true, to_apply=%region_6.7 | all-reduce | flops 3973 | bytes 31784 | tf_op jit(solution)/shard_map/psum | solution.py:225
  580.3 19.1 %psum.75 = f32[64,180]{1,0:T(8,128)S(1)} all-reduce(f32[64,180]{1,0:T(8,128)} %reduce-scatter.7.cloned.1.call-done), channel_id=1, replica_groups=mesh['dp'=4,'fsdp'=8] {'dp'}, use_global_device_ids=true, to_apply=%region_22.23 | all-reduce | flops 11520 | bytes 92160 | tf_op jit(solution)/shard_map/psum | solution.py:209
  600.0 43.7 %all-reduce.9.cloned.1.call-done = (f32[450,64]{0,1:T(8,128)}, f32[4,512,64]{1,2,0:T(8,128)}, f32[3600,64]{0,1:T(8,128)}, f32[64,720]{1,0:T(8,128)}) async-done(((f32[450,64]{0,1:T(8,128)}, f32[4,512,64]{1,2,0:T(8,128)}, f32[3600,64]{0,1:T(8,128)}, f32[64,720]{1,0:T(8,128)}), (f32[450,64]{0,1:T(8,128)}, f32[4,512,64]{1,2,0:T(8,128)}, f32[3600,64]{0,1:T(8,128)}, ...) | async-done | bytes 1745424 | tf_op jit(solution)/shard_map/psum | solution.py:209
  655.3 16.9 %psum.78 = f32[]{:T(128)} all-reduce(f32[]{:T(128)S(6)} %add.391), channel_id=1, replica_groups=mesh['dp'=4,'fsdp'=8] {'fsdp'}, use_global_device_ids=true, to_apply=%region_30.31 | all-reduce | flops 1 | bytes 8 | tf_op jit(solution)/shard_map/psum | solution.py:229
  (232 shorter events, 104.2 us)
Async XLA Ops:
  7.2 148.0 %all-gather.3.cloned.1.call-start = ((), (), s32[]{:S(2)}) async-start(), calls=%async_computation.4 | async-start | bytes 2359296 | tf_op jit(solution)/shard_map/all_gather | solution.py:176
  9.0 181.9 %all-gather.5.cloned.1.call-start = ((), (), s32[]{:S(2)}) async-start(), calls=%async_computation.5 | async-start | bytes 4276224 | tf_op jit(solution)/shard_map/all_gather | solution.py:178
  11.1 378.8 %all-reduce.7.cloned.1.call-start = ((), (), s32[]{:S(2)}) async-start(), calls=%async_computation.10 | async-start | bytes 8388608
  99.1 56.1 %copy-start.33 = (f32[24]{0:T(128)}, f32[24]{0:T(128)S(1)}, u32[]{:S(2)}) copy-start(f32[24]{0:T(128)S(1)} %get-tuple-element.158) | copy-start | bytes 292
  99.1 56.1 %copy-start.35 = (f32[24]{0:T(128)}, f32[24]{0:T(128)S(1)}, u32[]{:S(2)}) copy-start(f32[24]{0:T(128)S(1)} %get-tuple-element.159) | copy-start | bytes 292
  100.5 54.7 %copy-start.37 = (f32[24]{0:T(128)}, f32[24]{0:T(128)S(1)}, u32[]{:S(2)}) copy-start(f32[24]{0:T(128)S(1)} %fusion.42) | copy-start | bytes 292
  118.3 45.8 %copy-start.11 = (bf16[512,180]{1,0:T(8,128)(2,1)}, bf16[512,180]{1,0:T(8,128)(2,1)S(1)}, u32[]{:S(2)}) copy-start(bf16[512,180]{1,0:T(8,128)(2,1)S(1)} %all_gather.17) | copy-start | bytes 552964
  133.6 25.3 %copy-start.44 = (f32[512]{0:T(512)}, f32[512]{0:T(512)S(1)}, u32[]{:S(2)}) copy-start(f32[512]{0:T(512)S(1)} %get-tuple-element.133) | copy-start | bytes 6148
  293.8 130.7 %reduce-scatter.5.cloned.1.call-start = ((), (), s32[]{:S(2)}) async-start(), calls=%async_computation.6 | async-start | bytes 1179648 | tf_op jit(solution)/shard_map/reduce_scatter | solution.py:203
  301.9 157.3 %reduce-scatter.11.cloned.1.call-start = ((), (), s32[]{:S(2)}) async-start(), calls=%async_computation.9 | async-start | bytes 1769472 | tf_op jit(solution)/shard_map/reduce_scatter | solution.py:207
  309.9 231.5 %reduce-scatter.9.cloned.1.call-start = ((), (), s32[]{:S(2)}) async-start(), calls=%async_computation.8 | async-start | bytes 8552448 | tf_op jit(solution)/shard_map/reduce_scatter | solution.py:206
  324.9 216.7 %copy-start.26 = (f32[720]{0:T(1024)S(1)}, f32[720]{0:T(1024)}, u32[]{:S(2)}) copy-start(f32[720]{0:T(1024)} %get-tuple-element.119) | copy-start | bytes 8644
  324.9 216.7 %copy-start.39 = (f32[512]{0:T(512)S(1)}, f32[512]{0:T(512)}, u32[]{:S(2)}) copy-start(f32[512]{0:T(512)} %get-tuple-element.152) | copy-start | bytes 6148
  324.9 255.3 %reduce-scatter.7.cloned.1.call-start = ((), (), s32[]{:S(2)}) async-start(), calls=%async_computation.7 | async-start | bytes 589824 | tf_op jit(solution)/shard_map/reduce_scatter | solution.py:205
  328.0 345.5 %copy-start.25 = (f32[3972]{0:T(1024)S(1)}, f32[3972]{0:T(1024)}, u32[]{:S(2)}) copy-start(f32[3972]{0:T(1024)} %param.33) | copy-start | bytes 47668
  328.0 347.1 %copy-start.20 = (f32[64,180]{1,0:T(8,128)S(1)}, f32[64,180]{1,0:T(8,128)}, u32[]{:S(2)}) copy-start(f32[64,180]{1,0:T(8,128)} %param.30) | copy-start | bytes 138244
  328.0 348.7 %copy-start.18 = (f32[450,64]{0,1:T(8,128)S(1)}, f32[450,64]{0,1:T(8,128)}, u32[]{:S(2)}) copy-start(f32[450,64]{0,1:T(8,128)} %param.28) | copy-start | bytes 345604
  328.0 348.7 %copy-start.21 = (f32[450,64]{0,1:T(8,128)S(1)}, f32[450,64]{0,1:T(8,128)}, u32[]{:S(2)}) copy-start(f32[450,64]{0,1:T(8,128)} %param.34) | copy-start | bytes 345604
  328.1 350.4 %copy-start.16 = (f32[64,720]{1,0:T(8,128)S(1)}, f32[64,720]{1,0:T(8,128)}, u32[]{:S(2)}) copy-start(f32[64,720]{1,0:T(8,128)} %param.32) | copy-start | bytes 552964
  328.1 315.6 %all-reduce.9.cloned.1.call-start = ((), (), s32[]{:S(2)}) async-start(), calls=%async_computation.11 | async-start | bytes 3604480 | tf_op jit(solution)/shard_map/psum | solution.py:209
  391.0 289.5 %copy-start.8 = (f32[4,512,64]{1,2,0:T(8,128)S(1)}, f32[4,512,64]{1,2,0:T(8,128)}, u32[]{:S(2)}) copy-start(f32[4,512,64]{1,2,0:T(8,128)} %param.29) | copy-start | bytes 1572868
  600.0 83.1 %copy-start.5 = (f32[3600,64]{0,1:T(8,128)S(1)}, f32[3600,64]{0,1:T(8,128)}, u32[]{:S(2)}) copy-start(f32[3600,64]{0,1:T(8,128)} %param.31) | copy-start | bytes 2764804
  643.7 36.8 %copy-start.9 = (f32[4,512,64]{1,2,0:T(8,128)S(1)}, f32[4,512,64]{1,2,0:T(8,128)}, u32[]{:S(2)}) copy-start(f32[4,512,64]{1,2,0:T(8,128)} %get-tuple-element.98) | copy-start | bytes 1572868
  643.7 39.4 %copy-start.4 = (f32[3600,64]{0,1:T(8,128)S(1)}, f32[3600,64]{0,1:T(8,128)}, u32[]{:S(2)}) copy-start(f32[3600,64]{0,1:T(8,128)} %get-tuple-element.99) | copy-start | bytes 2764804
  (50 other events, 378.4 us)
Sparse Core Ops, SparseCore 0:
  10.2 31.7 all-gather.2
  44.3 43.9 all-gather.4
  293.9 95.9 all-reduce.6
  392.1 32.4 reduce-scatter.4
  426.7 32.4 reduce-scatter.10
  461.4 79.9 reduce-scatter.8
  544.2 29.3 reduce-scatter.6
  578.1 65.5 all-reduce.8
where the time goes:
time: 703 us; the launch traced here: 694 us
  waiting for transfers between devices  254 us (36%)
  blocking collectives  164 us (23%)
  other arithmetic  118 us (17%)
  matrix products  110 us (16%)
  local copies, waits for them, and re-layouts  25.2 us (4%)
  between operations  21.9 us (3%)
    reduce_scatter x1, waiting for transfers between devices, body(): lax.psum_scatter(grads[3], 'fsdp', scatter_dimension=1, tiled=True)  82.2 us
    unnamed x9, waiting for transfers between devices  60.7 us
    psum x1, blocking collectives, body(): table = lax.psum(local_table, ('dp', 'fsdp'))  43.8 us
    psum x1, waiting for transfers between devices, body(): lax.psum((partial_grads[0], partial_grads[1], partial_grads[2], partial_g...  43.7 us
    psum x1, blocking collectives, body(): bias_grad, loss_sum = lax.psum((bias_local, local_loss), ('dp', 'fsdp'))  38.5 us
    dot_general x7, matrix products, back_block(): lax.dot_general(rounded, mats[layer_at], (((1,), (1,)), ((), ())), prefer...  36.1 us
    dot_general x8, matrix products, run_block(): jnp.dot(lowered, mats[layer_at], preferred_element_type=jnp.float32)  34.9 us
    reduce_scatter x1, waiting for transfers between devices, body(): lax.psum_scatter(grads[4], 'fsdp', scatter_dimension=0, tiled=True)  34.7 us
  transfers between devices with their start and end apart: 8, of which 5 were waited for; matrix products, arithmetic and copies ran while one was open for 18% of the time, Pallas kernels for 0%

commit v1 on v0

v1 whole, which is shorter than its diff:
```python
import jax
import jax.numpy as jnp
import numpy as np
from jax import lax
from jax.experimental import pallas as pl
from jax.experimental.pallas import tpu as pltpu
from jax.sharding import PartitionSpec as P

LOOKBACK = 3600
OUTLOOK = 720
HID = 512
SERIES = 1024
STEP = 10
LP = 450
BACK = 150
FORE = 30
RATIO = 24
beta_first = 0.9
beta_second = 0.999
learn_rate = 0.01
weight_decay = 0.01
adam_epsilon = 1e-08
clip_level = 0.01

C_IN, C_M0, C_M1, C_OUT, C_ALL = 0, 512, 1024, 1536, 1792
F_IN, F_M2, F_M3, F_OUT, F_ALL = 0, 3840, 4352, 4864, 5632
T_PAD = 3840
T_LIVE = 3712
T_WHOLE = 3584
O_PAD = 768
TILE = 256
CINV_AT = 180

F32 = jnp.float32
BF16 = jnp.bfloat16
NN = (((1,), (0,)), ((), ()))
NT = (((1,), (1,)), ((), ()))
TN = (((0,), (0,)), ((), ()))


def mm(a, b, dims=NN):
    return lax.dot_general(a, b, dims, preferred_element_type=F32)


def iota(shape, axis):
    return lax.broadcasted_iota(jnp.int32, shape, axis)


def split3(v):
    hi = v.astype(BF16)
    rest = v - hi.astype(F32)
    mid = rest.astype(BF16)
    return hi, mid, (rest - mid.astype(F32)).astype(BF16)


def mm_exact(v, sel, dims=NN):
    hi, mid, low = split3(v)
    return mm(hi, sel, dims) + mm(mid, sel, dims) + mm(low, sel, dims)


def mm_exact2(sel, v, dims=NN):
    hi, mid, low = split3(v)
    return mm(sel, hi, dims) + mm(sel, mid, dims) + mm(sel, low, dims)


def sigmoid(v):
    return 1.0 / (1.0 + jnp.exp(-v))


def silu(v):
    return v * sigmoid(v)


def silu_slope(v):
    s = sigmoid(v)
    return s * (1.0 + v * (1.0 - s))


def vmem(limit=60):
    return pltpu.CompilerParams(vmem_limit_bytes=limit * 1024 * 1024)


def bits_of(size):
    return [1 << b for b in range(size.bit_length() - 1)]


def swap(x, dp, fsdp, bit_dp, bit_fsdp):
    pairs = []
    for d in range(dp):
        for f in range(fsdp):
            pairs.append((d * fsdp + f, (d ^ bit_dp) * fsdp + (f ^ bit_fsdp)))
    return lax.ppermute(x, ("dp", "fsdp"), pairs)


def gather_rows(x, dp, fsdp, swap_fn, join):
    far = bits_of(fsdp)
    for bit in reversed(far[1:]):
        x = join(x, swap_fn(x, 0, bit))
    half = x.shape[0] // 2
    a, b = x[:half], x[half:]
    for first, second in zip(reversed(bits_of(dp)), bits_of(dp)):
        a2 = swap_fn(a, first, 0)
        b2 = swap_fn(b, second, 0)
        a, b = join(a, a2), join(b, b2)
    x = join(a, b)
    return join(x, swap_fn(x, 0, far[0]))


def row_order(dp, fsdp):
    share = HID // fsdp
    part = share // dp
    start = np.arange(part)

    def shifted(x, bit_dp, bit_fsdp):
        return x ^ (bit_fsdp * share + bit_dp * part)

    return gather_rows(
        start, dp, fsdp, shifted, lambda p, q: np.concatenate([p, q])
    )


def pack_kernel(d_ref, cin, mid, cout, fin, fout, wc, wf):
    share = cout.shape[0]
    part = wc.shape[0]
    rows = max(part, 16)
    sel = (iota((rows, share), 1) == d_ref[0] * part + iota((rows, share), 0)).astype(BF16)
    wc[...] = jnp.zeros_like(wc)
    wf[...] = jnp.zeros_like(wf)

    def put(ref, at, value):
        picked = mm(sel, value.astype(BF16))
        ref[:, at : at + value.shape[1]] = picked[:part].astype(BF16)

    put(wc, C_IN, cin[...])
    put(wc, C_M0, mid[0])
    put(wc, C_M1, mid[1])
    put(wc, C_OUT, cout[...])
    put(wf, F_IN, fin[...])
    put(wf, F_M2, mid[2])
    put(wf, F_M3, mid[3])
    put(wf, F_OUT, fout[...])


def stats_kernel(hist, lens, series, pooled, table):
    cols = hist.shape[1]

    @pl.when(pl.program_id(0) == 0)
    def _():
        table[...] = jnp.zeros_like(table)

    begin = LOOKBACK - lens[...]
    sums = jnp.zeros((8, cols), F32)
    squares = jnp.zeros((8, cols), F32)
    chunk = 32
    base = iota((chunk, cols), 0) * 8
    for g in range(0, LP - chunk + 1, chunk):
        total = jnp.zeros((chunk, cols), F32)
        for s in range(8):
            h = hist[pl.ds(g * 8 + s, chunk, stride=8), :]
            h = jnp.where(base >= begin - (g * 8 + s), h, 0.0)
            total += h
            sq = h * h
            for v in range(chunk // 8):
                squares += sq[v * 8 : v * 8 + 8]
        for v in range(chunk // 8):
            sums += total[v * 8 : v * 8 + 8]
        pooled[g : g + chunk, :] = total * 0.125
    at = LP // chunk * chunk
    rest = LP - at
    pooled[at:HID, :] = jnp.zeros((HID - at, cols), F32)
    total = jnp.zeros((rest, cols), F32)
    rest_squares = jnp.zeros((rest, cols), F32)
    for s in range(8):
        h = hist[pl.ds(at * 8 + s, rest, stride=8), :]
        h = jnp.where(iota((rest, cols), 0) * 8 >= begin - (at * 8 + s), h, 0.0)
        total += h
        rest_squares += h * h
    pooled[at:LP, :] = total * 0.125
    sum_row = jnp.sum(sums, 0, keepdims=True) + jnp.sum(total, 0, keepdims=True)
    square_row = jnp.sum(squares, 0, keepdims=True) + jnp.sum(rest_squares, 0, keepdims=True)
    row = iota((16, cols), 0)
    kind = row % 3
    v = jnp.where(
        kind == 0, sum_row, jnp.where(kind == 1, square_row, lens[...].astype(F32))
    )
    hi, mid, low = split3(v)
    piece = jnp.where(
        row < 3,
        hi.astype(F32),
        jnp.where(row < 6, mid.astype(F32), jnp.where(row < 9, low.astype(F32), 0.0)),
    ).astype(BF16)
    hot = (iota((SERIES, cols), 0) == series[...]).astype(BF16)
    t = mm(piece, hot, NT)
    table[0:3, :] += t[0:3] + t[3:6] + t[6:9]


def coarse_kernel(p_in, lens, series, table, wc, offs, abscol, z_out, pooled_out, th_out,
                  look_out, looker, m0, m1, w_out, offs_p):
    cols = p_in.shape[1]

    @pl.when(pl.program_id(0) == 0)
    def _():
        perm = (iota((HID, HID), 1) == abscol[...]).astype(BF16)
        m0[...] = mm(wc[:, C_M0 : C_M0 + HID], perm, NT).astype(BF16)
        m1[...] = mm(wc[:, C_M1 : C_M1 + HID], perm, NT).astype(BF16)
        eye = (iota((256, 256), 0) == iota((256, 256), 1)).astype(BF16)
        w_out[...] = mm(eye, wc[:, C_OUT:C_ALL], NT).astype(BF16)
        offs_p[...] = mm_exact2(perm, offs[0:HID, :])
        count = jnp.maximum(table[2:3, :], 1.0)
        centre = table[0:1, :] / count
        spread = jnp.sqrt(table[1:2, :] / count + 1e-05)
        inverse = 1.0 / spread
        shifted = centre / spread
        row = iota((16, SERIES), 0)
        v = jnp.where(row < 3, inverse, shifted)
        hi, mid, low = split3(v)
        kind = row % 3
        looker[...] = jnp.where(
            row < 6,
            jnp.where(
                kind == 0,
                hi.astype(F32),
                jnp.where(kind == 1, mid.astype(F32), low.astype(F32)),
            ),
            0.0,
        ).astype(BF16)

    hot = (iota((SERIES, cols), 0) == series[...]).astype(BF16)
    got = mm(looker[...], hot)
    inv = got[0:1] + got[1:2] + got[2:3]
    cinv = got[3:4] + got[4:5] + got[5:6]
    look_out[...] = jnp.where(iota((8, cols), 0) == 0, inv, cinv)
    group = iota((HID, cols), 0)
    begin = LOOKBACK - lens[...]
    share = jnp.clip(group * 8 + 8 - begin, 0, 8).astype(F32) * 0.125
    pooled = jnp.where(group < LP, p_in[...] * inv - cinv * share, 0.0).astype(BF16)
    pooled_out[...] = pooled
    z = mm(wc[:, C_IN : C_IN + HID], pooled) + offs_p[:, 0:1]
    z_out[0:HID, :] = z
    z = mm(m0[...], silu(z).astype(BF16)) + offs_p[:, 1:2]
    z_out[HID : 2 * HID, :] = z
    z = mm(m1[...], silu(z).astype(BF16)) + offs_p[:, 2:3]
    z_out[2 * HID : 3 * HID, :] = z
    theta = mm(w_out[...], silu(z).astype(BF16)) + offs[0:256, 3:4]
    theta = theta * (1.0 / 48.0)
    hi = theta.astype(BF16).astype(F32)
    at = iota((256, cols), 0)
    c_hi, c_mid, c_low = split3(cinv)
    with_shift = jnp.where(
        at == CINV_AT,
        c_hi.astype(F32),
        jnp.where(
            at == CINV_AT + 1,
            c_mid.astype(F32),
            jnp.where(at == CINV_AT + 2, c_low.astype(F32), hi),
        ),
    )
    th_out[0:256, :] = with_shift.astype(BF16)
    th_out[256:512, :] = (theta - hi).astype(BF16)


def fold_lanes(x):
    total = x[:, 0:128]
    for at in range(128, x.shape[1], 128):
        total = total + x[:, at : at + 128]
    return total


def hidden_rows(acc, perm):
    lane = iota((HID, 128), 1)
    v = jnp.zeros((HID, 128), F32)
    for k in range(3):
        v = jnp.where(lane == k, jnp.sum(acc[k], 1, keepdims=True), v)
    return mm_exact(v, perm, TN)[0:8]


def last_row(acc):
    v = jnp.broadcast_to(jnp.sum(acc, 1, keepdims=True), acc.shape)
    return jnp.transpose(v, (1, 0))[0:8]


def fine_kernel(hist, later, flags, look, lens, th, wf, btab_t, ftab, ftab_t, offs, abscol,
                dz1_out, fore_out, keep, send, small,
                res, a1, a2, a3, dz1, dz2, dz3, dz4, m2, m3, m2_t, m3_t, w_out, offs_p, perm,
                acc, acc4, acc_loss, grad):
    cols = hist.shape[1]
    tiles = res.shape[1] // cols
    step = pl.program_id(0)

    @pl.when(step == 0)
    def _():
        p = (iota((HID, HID), 1) == abscol[...]).astype(BF16)
        perm[...] = p
        m2[...] = mm(wf[:, F_M2 : F_M2 + HID], p, NT).astype(BF16)
        m3[...] = mm(wf[:, F_M3 : F_M3 + HID], p, NT).astype(BF16)
        m2_t[...] = mm(p, wf[:, F_M2 : F_M2 + HID], NT).astype(BF16)
        m3_t[...] = mm(p, wf[:, F_M3 : F_M3 + HID], NT).astype(BF16)
        eye = (iota((256, 256), 0) == iota((256, 256), 1)).astype(BF16)
        for lo in range(0, O_PAD, 256):
            w_out[lo : lo + 256, :] = mm(
                eye, wf[:, F_OUT + lo : F_OUT + lo + 256], NT
            ).astype(BF16)
        offs_p[...] = mm_exact2(p, offs[0:HID, :])
        acc[...] = jnp.zeros_like(acc)
        acc4[...] = jnp.zeros_like(acc4)
        acc_loss[...] = jnp.zeros_like(acc_loss)
        res[LOOKBACK:T_PAD, :] = jnp.zeros((T_PAD - LOOKBACK, res.shape[1]), BF16)
        dz4[OUTLOOK:O_PAD, :] = jnp.zeros((O_PAD - OUTLOOK, dz4.shape[1]), BF16)

    @pl.when(step < tiles)
    def _():
        here = pl.ds(pl.multiple_of(step * cols, cols), cols)
        inv = look[0:1, :]
        cinv = look[1:2, :]
        begin = LOOKBACK - lens[...]
        th_hi = th[0:256, :]
        for lo in range(0, LOOKBACK, 512):
            width = min(512, LOOKBACK - lo)
            shift = mm(btab_t[lo : lo + width, :], th_hi)
            seen = iota((width, cols), 0) >= begin - lo
            r = jnp.where(seen, hist[lo : lo + width, :] * inv - shift, 0.0)
            res[lo : lo + width, here] = r.astype(BF16)
        z1 = mm(wf[:, F_IN : F_IN + T_LIVE], res[0:T_LIVE, here]) + offs_p[:, 0:1]
        v1 = silu(z1).astype(BF16)
        a1[:, here] = v1
        z2 = mm(m2[...], v1) + offs_p[:, 1:2]
        v2 = silu(z2).astype(BF16)
        a2[:, here] = v2
        z3 = mm(m3[...], v2) + offs_p[:, 2:3]
        v3 = silu(z3).astype(BF16)
        a3[:, here] = v3
        est = (
            mm(w_out[...], v3)
            + mm(ftab_t[...], th_hi)
            + mm(ftab_t[...], th[256:512, :])
            + offs[:, 3:4]
        )
        counted = flags[...].astype(F32)
        err = (est[0:OUTLOOK] - (later[...] * inv - cinv)) * counted
        acc_loss[0:1, :] += jnp.sum(err * err, 0, keepdims=True)
        acc_loss[1:2, :] += jnp.sum(counted, 0, keepdims=True)
        d4 = (2.0 * err).astype(BF16)
        acc4[0:OUTLOOK, :] += fold_lanes(d4.astype(F32))
        dz4[0:OUTLOOK, here] = d4
        d4 = dz4[:, here]
        fore_out[...] = mm(ftab[...], d4) * (1.0 / 48.0)

        def back(upstream, z, slot, row):
            d = (upstream * silu_slope(z)).astype(BF16)
            acc[row] += fold_lanes(d.astype(F32))
            slot[:, here] = d
            return d

        d3 = back(mm(wf[:, F_OUT:F_ALL], d4), z3, dz3, 2)
        d2 = back(mm(m3_t[...], d3), z2, dz2, 1)
        dz1_out[...] = back(mm(m2_t[...], d2), z1, dz1, 0)

    emit_tiles(step - tiles, keep, send, grad, perm, T_PAD // TILE,
               (dz1, res), (dz2, a1), (dz3, a2), (a3, dz4))

    @pl.when(step == pl.num_programs(0) - 1)
    def _():
        small[...] = last_row(acc4[...])
        loss = jnp.sum(acc_loss[0:1, :], 1, keepdims=True)
        tally = jnp.sum(acc_loss[1:2, :], 1, keepdims=True)
        row = iota((8, O_PAD), 0)
        small[...] = jnp.where(
            row == 3,
            small[...],
            jnp.where(row == 4, loss, jnp.where(row == 5, tally, 0.0)),
        )
        small[0:3, 0:HID] = hidden_rows(acc, perm[...])[0:3]


def emit_tiles(at, keep, send, grad, perm, in_tiles, first, second, third, fourth):
    half = HID // 2

    def emit(g):
        keep[...] = g[0:half]
        send[...] = g[half:HID].astype(BF16)

    @pl.when((at >= 0) & (at < in_tiles))
    def _():
        lo = pl.multiple_of(at * TILE, TILE)
        emit(mm(first[0][...], first[1][pl.ds(lo, TILE), :], NT))

    for index, (lhs, rhs) in enumerate((second, third)):

        @pl.when(at == in_tiles + 2 * index)
        def _():
            hi, mid, low = split3(mm(lhs[...], rhs[...], NT))
            grad[0] = hi
            grad[1] = mid
            grad[2] = low

        @pl.when((at >= in_tiles + 2 * index) & (at < in_tiles + 2 * index + 2))
        def _():
            lo = pl.multiple_of((at - in_tiles - 2 * index) * TILE, TILE)
            p = perm[:, pl.ds(lo, TILE)]
            emit(mm(grad[0], p) + mm(grad[1], p) + mm(grad[2], p))

    @pl.when(at >= in_tiles + 4)
    def _():
        lo = pl.multiple_of((at - in_tiles - 4) * TILE, TILE)
        emit(mm(fourth[0][...], fourth[1][pl.ds(lo, TILE), :], NT))


def back_kernel(dz1f, fore, lens, z, pooled_in, wf, btab, wc, abscol,
                keep, send, small,
                pooled, a1, a2, a3, dz1, dz2, dz3, dz4, w_in, m0_t, m1_t, perm, acc, acc4, grad):
    cols = dz1f.shape[1]
    tiles = pooled.shape[1] // cols
    step = pl.program_id(0)

    @pl.when(step == 0)
    def _():
        p = (iota((HID, HID), 1) == abscol[...]).astype(BF16)
        perm[...] = p
        m0_t[...] = mm(p, wc[:, C_M0 : C_M0 + HID], NT).astype(BF16)
        m1_t[...] = mm(p, wc[:, C_M1 : C_M1 + HID], NT).astype(BF16)
        eye = (iota((256, 256), 0) == iota((256, 256), 1)).astype(BF16)
        for lo in range(0, T_PAD, 256):
            w_in[lo : lo + 256, :] = mm(eye, wf[:, lo : lo + 256], NT).astype(BF16)
        acc[...] = jnp.zeros_like(acc)
        acc4[...] = jnp.zeros_like(acc4)

    @pl.when(step < tiles)
    def _():
        here = pl.ds(pl.multiple_of(step * cols, cols), cols)
        begin = LOOKBACK - lens[...]
        d1f = dz1f[...]
        total = jnp.zeros((256, cols), F32)
        for lo in range(0, T_LIVE, 512):
            width = min(512, T_LIVE - lo)
            d = mm(w_in[lo : lo + width, :], d1f)
            seen = iota((width, cols), 0) >= begin - lo
            d = jnp.where(seen, d, 0.0).astype(BF16)
            total += mm(btab[:, lo : lo + width], d)
        row = iota((256, cols), 0)
        d4 = (jnp.where(row < BACK, total * (-1.0 / 48.0), 0.0) + fore[...]).astype(BF16)
        dz4[:, here] = d4
        acc4[...] += fold_lanes(d4.astype(F32))
        pooled[:, here] = pooled_in[...]
        z1 = z[0:HID, :]
        z2 = z[HID : 2 * HID, :]
        z3 = z[2 * HID : 3 * HID, :]
        a1[:, here] = silu(z1).astype(BF16)
        a2[:, here] = silu(z2).astype(BF16)
        a3[:, here] = silu(z3).astype(BF16)

        def back(upstream, zz, slot, row):
            d = (upstream * silu_slope(zz)).astype(BF16)
            acc[row] += fold_lanes(d.astype(F32))
            slot[:, here] = d
            return d

        d3 = back(mm(wc[:, C_OUT:C_ALL], d4), z3, dz3, 2)
        d2 = back(mm(m1_t[...], d3), z2, dz2, 1)
        back(mm(m0_t[...], d2), z1, dz1, 0)

    emit_tiles(step - tiles, keep, send, grad, perm, HID // TILE,
               (dz1, pooled), (dz2, a1), (dz3, a2), (a3, dz4))

    @pl.when(step == pl.num_programs(0) - 1)
    def _():
        small[...] = jnp.zeros_like(small)
        small[0:3, :] = hidden_rows(acc, perm[...])[0:3]
        small[3:4, 0:256] = last_row(acc4[...])[0:1]


def adam_math(weight, mean_old, square_old, grad):
    mean_new = beta_first * mean_old + (1.0 - beta_first) * grad
    square_new = beta_second * square_old + (1.0 - beta_second) * grad * grad
    mean_hat = mean_new / (1.0 - beta_first**STEP)
    square_hat = square_new / (1.0 - beta_second**STEP)
    weight_new = weight - learn_rate * (
        mean_hat / (jnp.sqrt(square_hat) + adam_epsilon) + weight_decay * weight
    )
    return weight_new, mean_new, square_new


def adam_kernel(scale, gc, gf, relrow, *refs):
    ins, outs = refs[:15], refs[15:]
    share = gc.shape[0]
    s = scale[0, 0]
    place = (iota((share, share), 1) == relrow[...]).astype(BF16)

    def step(i, part, at, width, index):
        grad = mm_exact2(place, part[:, at : at + width], TN) * s
        old = [ins[i + 5 * k][index] for k in range(3)]
        for k, value in enumerate(adam_math(*old, grad)):
            outs[i + 5 * k][index] = value

    every = slice(None)
    step(0, gc, C_IN, LP, (every, every))
    step(1, gc, C_M0, HID, 0)
    step(1, gc, C_M1, HID, 1)
    step(1, gf, F_M2, HID, 2)
    step(1, gf, F_M3, HID, 3)
    step(2, gc, C_OUT, BACK + FORE, (every, every))
    step(4, gf, F_OUT, OUTLOOK, (every, every))
    for lo in range(0, LOOKBACK, 512):
        width = min(512, LOOKBACK - lo)
        step(3, gf, F_IN + lo, width, (every, slice(lo, lo + width)))


def interp_table(count, length, first_row, rows, cols):
    spots = np.clip((np.arange(length) + 0.5) * (count / length) - 0.5, 0.0, count - 1.0)
    table = np.maximum(0.0, 1.0 - np.abs(spots[None, :] - np.arange(count)[:, None]))
    out = np.zeros((rows, cols), np.float32)
    out[first_row : first_row + count, :length] = np.round(table * 48.0)
    return out


def spec(shape, index):
    return pl.BlockSpec(shape, index)


def fixed(shape):
    return pl.BlockSpec(shape, lambda i: (0,) * len(shape), pipeline_mode=pl.Buffered(1))


def whole_vmem(n):
    return [pl.BlockSpec(memory_space=pltpu.VMEM)] * n


def body(
    history, later_observed, lengths, counted_flags, series,
    coarse_in, middle, rough_final_matrix, fine_in, sharp_final_matrix, offset_vectors,
    coarse_in_mean, middle_mean, rough_final_first, fine_in_mean, sharp_final_first, biases_mean,
    coarse_in_square, middle_square, rough_final_second, fine_in_square, sharp_final_second,
    biases_square,
):
    dp, fsdp = lax.axis_size("dp"), lax.axis_size("fsdp")
    d_here, f_here = lax.axis_index("dp"), lax.axis_index("fsdp")
    rows = history.shape[0]
    share = HID // fsdp
    part = share // dp

    def exchange(x, bit_dp, bit_fsdp):
        return swap(x, dp, fsdp, bit_dp, bit_fsdp)

    def join(p, q):
        return jnp.concatenate([p, q], 0)

    here = f_here * share + d_here * part
    order = row_order(dp, fsdp)
    abscol = (jnp.asarray(order, jnp.int32) ^ here).reshape(HID, 1)

    wc_part, wf_part = pl.pallas_call(
        pack_kernel,
        out_shape=(
            jax.ShapeDtypeStruct((part, C_ALL), BF16),
            jax.ShapeDtypeStruct((part, F_ALL), BF16),
        ),
        in_specs=[pl.BlockSpec(memory_space=pltpu.SMEM)] + whole_vmem(5),
        out_specs=tuple(whole_vmem(2)),
        compiler_params=vmem(32),
        name="pack_weights",
    )(
        d_here.reshape(1),
        coarse_in.T,
        middle.transpose(0, 2, 1),
        rough_final_matrix,
        fine_in.T,
        sharp_final_matrix,
    )
    wc = gather_rows(wc_part, dp, fsdp, exchange, join)
    wf = gather_rows(wf_part, dp, fsdp, exchange, join)

    hist = history.T
    lens = lengths.reshape(1, rows)
    series_row = series.reshape(1, rows)
    r = 256
    tiles = rows // r
    last = tiles - 1

    def col_spec(height):
        return spec((height, r), lambda i: (0, jnp.minimum(i, last)))

    def out_spec():
        return spec((HID // 2, TILE), lambda i: (0, jnp.maximum(i - tiles, 0)))

    pooled_raw, table = pl.pallas_call(
        stats_kernel,
        grid=(rows // 128,),
        out_shape=(
            jax.ShapeDtypeStruct((HID, rows), F32),
            jax.ShapeDtypeStruct((8, SERIES), F32),
        ),
        in_specs=[spec((h, 128), lambda i: (0, i)) for h in (LOOKBACK, 1, 1)],
        out_specs=(
            spec((HID, 128), lambda i: (0, i)),
            pl.BlockSpec((8, SERIES), lambda i: (0, 0)),
        ),
        compiler_params=vmem(40),
        name="window_stats",
    )(hist, lens, series_row)
    for bit in bits_of(fsdp):
        table = table + exchange(table, 0, bit)
    for bit in bits_of(dp):
        table = table + exchange(table, bit, 0)

    hidden = offset_vectors[: 6 * HID].reshape(6, HID)
    rough_bias = offset_vectors[6 * HID : 6 * HID + BACK + FORE]
    sharp_bias = offset_vectors[6 * HID + BACK + FORE :]

    def bias_cols(three, last, width):
        out = jnp.pad(three, ((0, 0), (0, width - HID)))
        out = join(out, jnp.pad(last, (0, width - last.shape[0]))[None])
        return jnp.pad(out, ((0, 4), (0, 0))).T

    coarse_offs = bias_cols(hidden[:3], rough_bias, HID)
    fine_offs = bias_cols(hidden[3:], sharp_bias, O_PAD)

    square = pltpu.VMEM((HID, HID), BF16)
    wide = pltpu.VMEM((HID, rows), BF16)
    z, pooled, th, look = pl.pallas_call(
        coarse_kernel,
        grid=(tiles,),
        out_shape=(
            jax.ShapeDtypeStruct((3 * HID, rows), F32),
            jax.ShapeDtypeStruct((HID, rows), BF16),
            jax.ShapeDtypeStruct((HID, rows), BF16),
            jax.ShapeDtypeStruct((8, rows), F32),
        ),
        in_specs=[
            col_spec(HID),
            col_spec(1),
            col_spec(1),
            fixed((8, SERIES)),
            fixed((HID, C_ALL)),
            fixed((HID, 8)),
            fixed((HID, 1)),
        ],
        out_specs=(col_spec(3 * HID), col_spec(HID), col_spec(HID), col_spec(8)),
        scratch_shapes=[
            pltpu.VMEM((16, SERIES), BF16),
            square,
            square,
            pltpu.VMEM((256, HID), BF16),
            pltpu.VMEM((HID, 8), F32),
        ],
        compiler_params=vmem(50),
        name="coarse_forward",
    )(pooled_raw, lens, series_row, table, wc, coarse_offs, abscol)

    back_table = interp_table(BACK, LOOKBACK, 0, 256, T_PAD)
    btab = jnp.asarray(back_table, BF16)
    back_table[CINV_AT : CINV_AT + 3, :LOOKBACK] = 1.0
    btab_t = jnp.asarray(back_table.T, BF16)
    fore_table = interp_table(FORE, OUTLOOK, BACK, 256, O_PAD)
    ftab = jnp.asarray(fore_table, BF16)
    ftab_t = jnp.asarray(fore_table.T, BF16)

    dz1f, fore, f_keep, f_send, f_small = pl.pallas_call(
        fine_kernel,
        grid=(tiles + F_ALL // TILE,),
        out_shape=(
            jax.ShapeDtypeStruct((HID, rows), BF16),
            jax.ShapeDtypeStruct((256, rows), F32),
            jax.ShapeDtypeStruct((HID // 2, F_ALL), F32),
            jax.ShapeDtypeStruct((HID // 2, F_ALL), BF16),
            jax.ShapeDtypeStruct((8, O_PAD), F32),
        ),
        in_specs=[
            col_spec(LOOKBACK),
            col_spec(OUTLOOK),
            col_spec(OUTLOOK),
            col_spec(8),
            col_spec(1),
            col_spec(HID),
            fixed((HID, F_ALL)),
            fixed((T_PAD, 256)),
            fixed((256, O_PAD)),
            fixed((O_PAD, 256)),
            fixed((O_PAD, 8)),
            fixed((HID, 1)),
        ],
        out_specs=(
            col_spec(HID),
            col_spec(256),
            out_spec(),
            out_spec(),
            pl.BlockSpec((8, O_PAD), lambda i: (0, 0)),
        ),
        scratch_shapes=[
            pltpu.VMEM((T_PAD, rows), BF16),
            wide, wide, wide, wide, wide, wide,
            pltpu.VMEM((O_PAD, rows), BF16),
            square, square, square, square,
            pltpu.VMEM((O_PAD, HID), BF16),
            pltpu.VMEM((HID, 8), F32),
            square,
            pltpu.VMEM((3, HID, 128), F32),
            pltpu.VMEM((O_PAD, 128), F32),
            pltpu.VMEM((8, r), F32),
            pltpu.VMEM((3, HID, HID), BF16),
        ],
        compiler_params=vmem(63),
        name="fine_block",
    )(
        hist, later_observed.T, counted_flags.T, look, lens, th,
        wf, btab_t, ftab, ftab_t, fine_offs, abscol,
    )

    c_keep, c_send, c_small = pl.pallas_call(
        back_kernel,
        grid=(tiles + C_ALL // TILE,),
        out_shape=(
            jax.ShapeDtypeStruct((HID // 2, C_ALL), F32),
            jax.ShapeDtypeStruct((HID // 2, C_ALL), BF16),
            jax.ShapeDtypeStruct((8, HID), F32),
        ),
        in_specs=[
            col_spec(HID),
            col_spec(256),
            col_spec(1),
            col_spec(3 * HID),
            col_spec(HID),
            fixed((HID, T_PAD)),
            fixed((256, T_PAD)),
            fixed((HID, C_ALL)),
            fixed((HID, 1)),
        ],
        out_specs=(out_spec(), out_spec(), pl.BlockSpec((8, HID), lambda i: (0, 0))),
        scratch_shapes=[
            wide, wide, wide, wide, wide, wide, wide,
            pltpu.VMEM((256, rows), BF16),
            pltpu.VMEM((T_PAD, HID), BF16),
            square, square, square,
            pltpu.VMEM((3, HID, 128), F32),
            pltpu.VMEM((256, 128), F32),
            pltpu.VMEM((3, HID, HID), BF16),
        ],
        compiler_params=vmem(60),
        name="coarse_backward",
    )(dz1f, fore, lens, z, pooled, wf, btab, wc, abscol)

    def step_sum(keep, send, bit_dp, bit_fsdp):
        return keep + exchange(send.astype(BF16), bit_dp, bit_fsdp).astype(F32)

    def halve(x, bit_dp, bit_fsdp):
        half = x.shape[0] // 2
        return step_sum(x[:half], x[half:], bit_dp, bit_fsdp)

    def scatter_rows(keep, send):
        far = bits_of(fsdp)
        x = step_sum(keep, send, 0, far[0])
        half = x.shape[0] // 2
        a, b = x[:half], x[half:]
        for first, second in zip(bits_of(dp), reversed(bits_of(dp))):
            a, b = halve(a, first, 0), halve(b, second, 0)
        x = join(a, b)
        for bit in far[1:]:
            x = halve(x, 0, bit)
        return x

    def share_rows(x):
        half = x.shape[0] // 2
        a, b = x[:half], x[half:]
        for first, second in zip(reversed(bits_of(dp)), bits_of(dp)):
            a2, b2 = exchange(a, first, 0), exchange(b, second, 0)
            a, b = join(a, a2), join(b, b2)
        return join(a, b)

    gf_part = scatter_rows(f_keep, f_send)
    gc_part = scatter_rows(c_keep, c_send)
    gf = share_rows(gf_part)
    gc = share_rows(gc_part)

    rel = np.arange(part)
    lo, hi = rel[: part // 2], rel[part // 2 :]
    for first, second in zip(reversed(bits_of(dp)), bits_of(dp)):
        lo = np.concatenate([lo, lo ^ (first * part)])
        hi = np.concatenate([hi, hi ^ (second * part)])
    relrow = (
        jnp.asarray(np.concatenate([lo, hi]), jnp.int32) ^ (d_here * part)
    ).reshape(share, 1)

    squares = jnp.sum(gf_part * gf_part) + jnp.sum(gc_part * gc_part)
    small = jnp.concatenate([f_small, c_small], 1)
    small = jnp.where(
        (iota(small.shape, 0) == 6) & (iota(small.shape, 1) == 0), squares, small
    )
    for bit in bits_of(dp):
        small = small + exchange(small, bit, 0)
    for bit in bits_of(fsdp):
        small = small + exchange(small, 0, bit)
    bias_sum = jnp.concatenate(
        [
            small[0:3, O_PAD : O_PAD + HID].reshape(-1),
            small[0:3, 0:HID].reshape(-1),
            small[3, O_PAD : O_PAD + BACK + FORE],
            small[3, 0:OUTLOOK],
        ]
    )
    loss_sum = small[4, 0]
    usable_tally = small[5, 0]
    total_square = small[6, 0] + jnp.sum(bias_sum * bias_sum)
    grad_norm = jnp.sqrt(total_square) / usable_tally
    factor = clip_level / jnp.maximum(grad_norm, clip_level)
    scale = factor / usable_tally

    def by_hidden(cin, mid, cout, fin, fout):
        return (cin.T, mid.transpose(0, 2, 1), cout, fin.T, fout)

    shards = (
        *by_hidden(coarse_in, middle, rough_final_matrix, fine_in, sharp_final_matrix),
        *by_hidden(
            coarse_in_mean, middle_mean, rough_final_first, fine_in_mean, sharp_final_first
        ),
        *by_hidden(
            coarse_in_square, middle_square, rough_final_second, fine_in_square,
            sharp_final_second,
        ),
    )
    new = pl.pallas_call(
        adam_kernel,
        out_shape=tuple(jax.ShapeDtypeStruct(x.shape, F32) for x in shards),
        in_specs=[pl.BlockSpec(memory_space=pltpu.SMEM)] + whole_vmem(18),
        out_specs=tuple(whole_vmem(15)),
        compiler_params=vmem(60),
        name="adam",
    )(scale.reshape(1, 1), gc, gf, relrow, *shards)
    bias_new = adam_math(offset_vectors, biases_mean, biases_square, bias_sum * scale)
    return (
        loss_sum, usable_tally, grad_norm,
        *by_hidden(*new[0:5]), bias_new[0],
        *by_hidden(*new[5:10]), bias_new[1],
        *by_hidden(*new[10:15]), bias_new[2],
    )


def solution(mesh):
    rows2 = P(("dp", "fsdp"), None)
    rows1 = P(("dp", "fsdp"))
    weights = (P(None, "fsdp"), P(None, None, "fsdp"), P("fsdp", None), P(None, "fsdp"), P("fsdp", None), P())
    in_specs = (rows2, rows2, rows1, rows2, rows1) + weights * 3
    out_specs = (P(), P(), P()) + weights * 3
    return jax.shard_map(body, mesh=mesh, in_specs=in_specs, out_specs=out_specs, check_vma=False)
```

time: 703 us -> 388 us (0.55); the launches traced: 694 us -> 387 us
  blocking collectives: 164 us -> 0 us
  Pallas kernels: 0 us -> 161 us
  waiting for transfers between devices: 254 us -> 123 us
  matrix products: 110 us -> 0 us
  other arithmetic: 118 us -> 9.62 us
  starting transfers between devices: 0.58 us -> 59.4 us
  between operations: 21.9 us -> 6.36 us
    pallas_call x0 -> x6, Pallas kernels: none -> 161 us  [the longest x1 77.2 us: body(): pl.pallas_call(fine_kernel, grid=(tiles + F_ALL // TILE,), out_shape=(jax...]
    reduce_scatter x4 -> x0, waiting for transfers between devices: 149 us -> none  [the longest x1 82.2 us: body(): lax.psum_scatter(grads[3], 'fsdp', scatter_dimension=1, tiled=True)]
    ppermute x0 -> x46, waiting for transfers between devices: none -> 123 us  [swap(): return lax.ppermute(x, ('dp', 'fsdp'), pairs)]
    psum x4 -> x0, blocking collectives: 118 us -> none  [the longest x1 43.8 us: body(): table = lax.psum(local_table, ('dp', 'fsdp'))]
    dot_general x25 -> x0, matrix products: 110 us -> none  [the longest x7 36.1 us: back_block(): lax.dot_general(rounded, mats[layer_at], (((1,), (1,)), ((), ())), prefer...]
    reduce_sum x13 -> x3, other arithmetic: 75.7 us -> 1.92 us  [the longest x2 1.32 us: body(): squares = jnp.sum(gf_part * gf_part) + jnp.sum(gc_part * gc_part)]
    unnamed x9 -> x0, waiting for transfers between devices: 60.7 us -> none
    ppermute x0 -> x46, starting transfers between devices: none -> 59.4 us  [swap(): return lax.ppermute(x, ('dp', 'fsdp'), pairs)]
  transfers between devices with their start and end apart: 8 -> 46, of which waited for: 5 -> 33; matrix products, arithmetic and copies ran while one was open for 18% -> 6% of each run, Pallas kernels for 0% -> 9%
where the time goes in v1:
time: 388 us; the launch traced here: 387 us
  Pallas kernels  161 us (41%)
  waiting for transfers between devices  123 us (32%)
  starting transfers between devices  59.4 us (15%)
  local copies, waits for them, and re-layouts  27.7 us (7%)
  other arithmetic  9.62 us (2%)
  between operations  6.36 us (2%)
    ppermute x46, waiting for transfers between devices, swap(): return lax.ppermute(x, ('dp', 'fsdp'), pairs)  123 us
    pallas_call x1, Pallas kernels, body(): pl.pallas_call(fine_kernel, grid=(tiles + F_ALL // TILE,), out_shape=(jax...  77.2 us
    ppermute x46, starting transfers between devices, swap(): return lax.ppermute(x, ('dp', 'fsdp'), pairs)  59.4 us
    pallas_call x1, Pallas kernels, body(): pl.pallas_call(back_kernel, grid=(tiles + C_ALL // TILE,), out_shape=(jax...  40.5 us
    pallas_call x1, Pallas kernels, body(): pl.pallas_call(stats_kernel, grid=(rows // 128,), out_shape=(jax.ShapeDty...  19.2 us
    unnamed x66, local copies, waits for them, and re-layouts  19.2 us
    pallas_call x1, Pallas kernels, body(): pl.pallas_call(coarse_kernel, grid=(tiles,), out_shape=(jax.ShapeDtypeStr...  17 us
  transfers between devices with their start and end apart: 46, of which 33 were waited for; matrix products, arithmetic and copies ran while one was open for 6% of the time, Pallas kernels for 9%

profile of v1, /device:TPU:0, one launch (start us, length us, event | category | flops | bytes accessed | tf_op | source)
XLA Modules:
  0.0 387.0 jit_solution(2362604649515485537)
XLA Ops:
  5.8 4.1 %collective-permute-start.12 = (bf16[16,5632]{1,0:T(8,128)(2,1)S(1)}, bf16[16,5632]{1,0:T(8,128)(2,1)S(1)}, u32[]{:S(2)}, u32[]{:S(2)}) collective-permute-start(bf16[16,5632]{1,0:T(8,128)(2,1)S(1)} %get-tuple-element.57), channel_id=1, source_target_pairs={{0,4},{1,5},{2,6},{3,7},{4,0},{5,1},{6,2},{7,3},{8,12},{9,13},{10,... | collective-permute-start | bytes 540680 | tf_op jit(solution)/shard_map/ppermute | solution.py:92
  10.7 9.5 %collective-permute-done.12 = bf16[16,5632]{1,0:T(8,128)(2,1)S(1)} collective-permute-done((bf16[16,5632]{1,0:T(8,128)(2,1)S(1)}, bf16[16,5632]{1,0:T(8,128)(2,1)S(1)}, u32[]{:S(2)}, u32[]{:S(2)}) %collective-permute-start.12) | collective-permute-done | bytes 180256 | tf_op jit(solution)/shard_map/ppermute | solution.py:92
  24.4 6.7 %collective-permute-done.13 = bf16[32,5632]{1,0:T(8,128)(2,1)S(1)} collective-permute-done((bf16[32,5632]{1,0:T(8,128)(2,1)S(1)}, bf16[32,5632]{1,0:T(8,128)(2,1)S(1)}, u32[]{:S(2)}, u32[]{:S(2)}) %collective-permute-start.13) | collective-permute-done | bytes 360480 | tf_op jit(solution)/shard_map/ppermute | solution.py:92
  34.6 18.8 %collective-permute-done.16 = bf16[32,5632]{1,0:T(8,128)(2,1)S(1)} collective-permute-done((bf16[32,5632]{1,0:T(8,128)(2,1)S(1)}, bf16[32,5632]{1,0:T(8,128)(2,1)S(1)}, u32[]{:S(2)}, u32[]{:S(2)}) %collective-permute-start.16) | collective-permute-done | bytes 360480 | tf_op jit(solution)/shard_map/ppermute | solution.py:92
  57.1 10.1 %collective-permute-done.17 = bf16[64,5632]{1,0:T(8,128)(2,1)S(1)} collective-permute-done((bf16[64,5632]{1,0:T(8,128)(2,1)S(1)}, bf16[64,5632]{1,0:T(8,128)(2,1)S(1)}, u32[]{:S(2)}, u32[]{:S(2)}) %collective-permute-start.17) | collective-permute-done | bytes 720928 | tf_op jit(solution)/shard_map/ppermute | solution.py:92
  68.2 4.3 %collective-permute-start.8 = (bf16[32,1792]{1,0:T(8,128)(2,1)S(1)}, bf16[32,1792]{1,0:T(8,128)(2,1)S(1)}, u32[]{:S(2)}, u32[]{:S(2)}) collective-permute-start(bf16[32,1792]{1,0:T(8,128)(2,1)S(1)} %get-tuple-element.138), channel_id=1, source_target_pairs={{0,2},{1,3},{2,0},{3,1},{4,6},{5,7},{6,4},{7,5},{8,10},{9,11},{10,... | collective-permute-start | bytes 344072 | tf_op jit(solution)/shard_map/ppermute | solution.py:92
  78.5 4.3 %collective-permute-done.9 = bf16[32,1792]{1,0:T(8,128)(2,1)S(1)} collective-permute-done((bf16[32,1792]{1,0:T(8,128)(2,1)S(1)}, bf16[32,1792]{1,0:T(8,128)(2,1)S(1)}, u32[]{:S(2)}, u32[]{:S(2)}) %collective-permute-start.9) | collective-permute-done | bytes 114720 | tf_op jit(solution)/shard_map/ppermute | solution.py:92
  86.4 3.3 collective-permute-done.10
  90.5 19.2 %window_stats.1 = (f32[512,2048]{1,0:T(8,128)S(1)}, f32[8,1024]{1,0:T(8,128)S(1)}) custom-call(f32[3600,2048]{1,0:T(8,128)} %bitcast.49, s32[1,2048]{1,0:T(1,128)S(1)} %bitcast.45, s32[1,2048]{1,0:T(1,128)S(1)} %bitcast.47), custom_call_target="tpu_custom_call" | custom-call | tf_op jit(solution)/shard_map/window_stats/pallas_call | solution.py:584
  113.3 3.7 collective-permute-done.1
  117.0 3.4 collective-permute-start.2
  130.2 17.0 %coarse_forward.1 = (f32[1536,2048]{1,0:T(8,128)}, bf16[512,2048]{1,0:T(8,128)(2,1)}, bf16[512,2048]{1,0:T(8,128)(2,1)}, f32[8,2048]{1,0:T(8,128)S(1)}) custom-call(f32[512,2048]{1,0:T(8,128)} %copy-done.2, s32[1,2048]{1,0:T(1,128)S(1)} %bitcast.46, s32[1,2048]{1,0:T(1,128)S(1)} %bitcast.48, f32[8,1024]{1,0:T(8,128)S(1)} %add.110.table, ...), custom_call_target="tpu_custom_call" | custom-call | tf_op jit(solution)/shard_map/coarse_forward/pallas_call | solution.py:618
  151.7 77.2 %fine_block.1 = (bf16[512,2048]{1,0:T(8,128)(2,1)}, f32[256,2048]{1,0:T(8,128)}, f32[256,5632]{1,0:T(8,128)}, bf16[256,5632]{1,0:T(8,128)(2,1)}, f32[8,768]{1,0:T(8,128)}) custom-call(f32[3600,2048]{1,0:T(8,128)} %bitcast.50, f32[720,2048]{1,0:T(8,128)} %bitcast.51, s32[720,2048]{1,0:T(8,128)} %bitcast.52, f32[8,2048]{1,0:T(8,128)} %copy-done.9, ...), custom_call_target="tpu_custom_call" | custom-call | tf_op jit(solution)/shard_map/fine_block/pallas_call | solution.py:656
  228.9 40.5 %coarse_backward.1 = (f32[256,1792]{1,0:T(8,128)}, bf16[256,1792]{1,0:T(8,128)(2,1)}, f32[8,512]{1,0:T(8,128)}) custom-call(bf16[512,2048]{1,0:T(8,128)(2,1)} %get-tuple-element.60.dz1f, f32[256,2048]{1,0:T(8,128)} %get-tuple-element.61.fore, s32[1,2048]{1,0:T(1,128)} %bitcast.44, f32[1536,2048]{1,0:T(8,128)} %get-tuple-element.62.z, ...), custom_call_target="tpu_custom_call" | custom-call | tf_op jit(solution)/shard_map/coarse_backward/pallas_call | solution.py:707
  277.0 4.6 %collective-permute-done.27 = bf16[64,1792]{1,0:T(8,128)(2,1)S(1)} collective-permute-done((bf16[64,1792]{1,0:T(8,128)(2,1)S(1)}, bf16[64,1792]{1,0:T(8,128)(2,1)S(1)}, u32[]{:S(2)}, u32[]{:S(2)}) %collective-permute-start.27) | collective-permute-done | bytes 229408 | tf_op jit(solution)/shard_map/ppermute | solution.py:92
  289.6 3.6 fusion.7
  301.2 8.0 %collective-permute-done.20 = bf16[64,5632]{1,0:T(8,128)(2,1)S(1)} collective-permute-done((bf16[64,5632]{1,0:T(8,128)(2,1)S(1)}, bf16[64,5632]{1,0:T(8,128)(2,1)S(1)}, u32[]{:S(2)}, u32[]{:S(2)}) %collective-permute-start.20) | collective-permute-done | bytes 720928 | tf_op jit(solution)/shard_map/ppermute | solution.py:92
  312.9 3.2 collective-permute-done.38
  321.0 3.6 collective-permute-done.21
  324.6 3.6 collective-permute-done.24
  332.2 4.5 %collective-permute-done.25 = bf16[16,5632]{1,0:T(8,128)(2,1)S(1)} collective-permute-done((bf16[16,5632]{1,0:T(8,128)(2,1)S(1)}, bf16[16,5632]{1,0:T(8,128)(2,1)S(1)}, u32[]{:S(2)}, u32[]{:S(2)}) %collective-permute-start.25) | collective-permute-done | bytes 180256 | tf_op jit(solution)/shard_map/ppermute | solution.py:92
  366.3 3.7 collective-permute-done.44
  371.2 6.5 %collective-permute-done.45 = f32[16,5632]{1,0:T(8,128)S(1)} collective-permute-done((f32[16,5632]{1,0:T(8,128)S(1)}, f32[16,5632]{1,0:T(8,128)S(1)}, u32[]{:S(2)}, u32[]{:S(2)}) %collective-permute-start.45) | collective-permute-done | bytes 360480 | tf_op jit(solution)/shard_map/ppermute | solution.py:92
  378.9 7.0 %adam.1 = (f32[64,450]{1,0:T(8,128)}, f32[4,64,512]{2,1,0:T(8,128)}, f32[64,180]{1,0:T(8,128)}, f32[64,3600]{1,0:T(8,128)}, f32[64,720]{1,0:T(8,128)}, /*index=5...) custom-call(f32[1,1]{1,0:T(1,128)} %bitcast.17.scale, ...), custom_call_target="tpu_custom_call" | custom-call | tf_op jit(solution)/shard_map/adam/pallas_call | solution.py:818
  (217 shorter events, 110.2 us)
Async XLA Ops:
  5.8 14.4 %collective-permute-start.12 = (bf16[16,5632]{1,0:T(8,128)(2,1)S(1)}, bf16[16,5632]{1,0:T(8,128)(2,1)S(1)}, u32[]{:S(2)}, u32[]{:S(2)}) collective-permute-start(bf16[16,5632]{1,0:T(8,128)(2,1)S(1)} %get-tuple-element.57), channel_id=1, source_target_pairs={{0,4},{1,5},{2,6},{3,7},{4,0},{5,1},{6,2},{7,3},{8,12},{9,13},{10,... | collective-permute-start | bytes 540680 | tf_op jit(solution)/shard_map/ppermute | solution.py:92
  9.9 13.2 %collective-permute-start.5 = (bf16[16,1792]{1,0:T(8,128)(2,1)S(1)}, bf16[16,1792]{1,0:T(8,128)(2,1)S(1)}, u32[]{:S(2)}, u32[]{:S(2)}) collective-permute-start(bf16[16,1792]{1,0:T(8,128)(2,1)S(1)} %get-tuple-element.54), channel_id=1, source_target_pairs={{0,4},{1,5},{2,6},{3,7},{4,0},{5,1},{6,2},{7,3},{8,12},{9,13},{10,... | collective-permute-start | bytes 172040 | tf_op jit(solution)/shard_map/ppermute | solution.py:92
  20.9 10.2 %collective-permute-start.13 = (bf16[32,5632]{1,0:T(8,128)(2,1)S(1)}, bf16[32,5632]{1,0:T(8,128)(2,1)S(1)}, u32[]{:S(2)}, u32[]{:S(2)}) collective-permute-start(bf16[32,5632]{1,0:T(8,128)(2,1)S(1)} %get-tuple-element.122), channel_id=1, source_target_pairs={{0,16},{1,17},{2,18},{3,19},{4,20},{5,21},{6,22},{7,23},{8,24},{9,... | collective-permute-start | bytes 1081352 | tf_op jit(solution)/shard_map/ppermute | solution.py:92
  23.7 48.9 %collective-permute-start.6 = (bf16[32,1792]{1,0:T(8,128)(2,1)S(1)}, bf16[32,1792]{1,0:T(8,128)(2,1)S(1)}, u32[]{:S(2)}, u32[]{:S(2)}) collective-permute-start(bf16[32,1792]{1,0:T(8,128)(2,1)S(1)} %get-tuple-element.138), channel_id=1, source_target_pairs={{0,16},{1,17},{2,18},{3,19},{4,20},{5,21},{6,22},{7,23},{8,24},{9,... | collective-permute-start | bytes 344072 | tf_op jit(solution)/shard_map/ppermute | solution.py:92
  24.2 8.4 %collective-permute-start.15 = (bf16[32,5632]{1,0:T(8,128)(2,1)S(1)}, bf16[32,5632]{1,0:T(8,128)(2,1)S(1)}, u32[]{:S(2)}, u32[]{:S(2)}) collective-permute-start(bf16[32,5632]{1,0:T(8,128)(2,1)S(1)} %get-tuple-element.122), channel_id=1, source_target_pairs={{0,2},{1,3},{2,0},{3,1},{4,6},{5,7},{6,4},{7,5},{8,10},{9,11},{10,... | collective-permute-start | bytes 1081352 | tf_op jit(solution)/shard_map/ppermute | solution.py:92
  31.1 23.4 %collective-permute-start.14 = (bf16[64,5632]{1,0:T(8,128)(2,1)S(1)}, bf16[64,5632]{1,0:T(8,128)(2,1)S(1)}, u32[]{:S(2)}, u32[]{:S(2)}) collective-permute-start(bf16[64,5632]{1,0:T(8,128)(2,1)S(1)} %pad_maximum_fusion), channel_id=1, source_target_pairs={{0,8},{1,9},{2,10},{3,11},{4,12},{5,13},{6,14},{7,15},{8,0},{9,1},... | collective-permute-start | bytes 2162696 | tf_op jit(solution)/shard_map/ppermute | solution.py:92
  32.6 20.9 %collective-permute-start.16 = (bf16[32,5632]{1,0:T(8,128)(2,1)S(1)}, bf16[32,5632]{1,0:T(8,128)(2,1)S(1)}, u32[]{:S(2)}, u32[]{:S(2)}) collective-permute-start(bf16[32,5632]{1,0:T(8,128)(2,1)S(1)} %collective-permute-done.15), channel_id=1, source_target_pairs={{0,8},{1,9},{2,10},{3,11},{4,12},{5,13},{6,14},{7,15},{8,0},{9,1},... | collective-permute-start | bytes 1081352 | tf_op jit(solution)/shard_map/ppermute | solution.py:92
  53.5 13.7 %collective-permute-start.17 = (bf16[64,5632]{1,0:T(8,128)(2,1)S(1)}, bf16[64,5632]{1,0:T(8,128)(2,1)S(1)}, u32[]{:S(2)}, u32[]{:S(2)}) collective-permute-start(bf16[64,5632]{1,0:T(8,128)(2,1)S(1)} %pad_maximum_fusion.1), channel_id=1, source_target_pairs={{0,16},{1,17},{2,18},{3,19},{4,20},{5,21},{6,22},{7,23},{8,24},{9,... | collective-permute-start | bytes 2162696 | tf_op jit(solution)/shard_map/ppermute | solution.py:92
  68.2 79.0 %collective-permute-start.18 = (bf16[256,5632]{1,0:T(8,128)(2,1)}, bf16[256,5632]{1,0:T(8,128)(2,1)}, u32[]{:S(2)}, u32[]{:S(2)}) collective-permute-start(bf16[256,5632]{1,0:T(8,128)(2,1)} %get-tuple-element.102), channel_id=1, source_target_pairs={{0,1},{1,0},{2,3},{3,2},{4,5},{5,4},{6,7},{7,6},{8,9},{9,8},{10,11... | collective-permute-start | bytes 8650760 | tf_op jit(solution)/shard_map/ppermute | solution.py:92
  68.2 8.1 %collective-permute-start.8 = (bf16[32,1792]{1,0:T(8,128)(2,1)S(1)}, bf16[32,1792]{1,0:T(8,128)(2,1)S(1)}, u32[]{:S(2)}, u32[]{:S(2)}) collective-permute-start(bf16[32,1792]{1,0:T(8,128)(2,1)S(1)} %get-tuple-element.138), channel_id=1, source_target_pairs={{0,2},{1,3},{2,0},{3,1},{4,6},{5,7},{6,4},{7,5},{8,10},{9,11},{10,... | collective-permute-start | bytes 344072 | tf_op jit(solution)/shard_map/ppermute | solution.py:92
  72.6 11.8 %collective-permute-start.7 = (bf16[64,1792]{1,0:T(8,128)(2,1)S(1)}, bf16[64,1792]{1,0:T(8,128)(2,1)S(1)}, u32[]{:S(2)}, u32[]{:S(2)}) collective-permute-start(bf16[64,1792]{1,0:T(8,128)(2,1)S(1)} %pad_maximum_fusion.4), channel_id=1, source_target_pairs={{0,8},{1,9},{2,10},{3,11},{4,12},{5,13},{6,14},{7,15},{8,0},{9,1},... | collective-permute-start | bytes 688136 | tf_op jit(solution)/shard_map/ppermute | solution.py:92
  90.4 39.7 %collective-permute-start.11 = (bf16[256,1792]{1,0:T(8,128)(2,1)}, bf16[256,1792]{1,0:T(8,128)(2,1)S(1)}, u32[]{:S(2)}, u32[]{:S(2)}) collective-permute-start(bf16[256,1792]{1,0:T(8,128)(2,1)} %get-tuple-element.116), channel_id=1, source_target_pairs={{0,1},{1,0},{2,3},{3,2},{4,5},{5,4},{6,7},{7,6},{8,9},{9,8},{10,11... | collective-permute-start | bytes 2752520 | tf_op jit(solution)/shard_map/ppermute | solution.py:92
  269.5 20.1 %collective-permute-start.19 = (bf16[256,5632]{1,0:T(8,128)(2,1)}, bf16[256,5632]{1,0:T(8,128)(2,1)S(1)}, u32[]{:S(2)}, u32[]{:S(2)}) collective-permute-start(bf16[256,5632]{1,0:T(8,128)(2,1)} %get-tuple-element.59), channel_id=1, source_target_pairs={{0,1},{1,0},{2,3},{3,2},{4,5},{5,4},{6,7},{7,6},{8,9},{9,8},{10,11... | collective-permute-start | bytes 8650760 | tf_op jit(solution)/shard_map/ppermute | solution.py:92
  274.0 7.7 %collective-permute-start.27 = (bf16[64,1792]{1,0:T(8,128)(2,1)S(1)}, bf16[64,1792]{1,0:T(8,128)(2,1)S(1)}, u32[]{:S(2)}, u32[]{:S(2)}) collective-permute-start(bf16[64,1792]{1,0:T(8,128)(2,1)S(1)} %get-tuple-element.101), channel_id=1, source_target_pairs={{0,8},{1,9},{2,10},{3,11},{4,12},{5,13},{6,14},{7,15},{8,0},{9,1},... | collective-permute-start | bytes 688136 | tf_op jit(solution)/shard_map/ppermute | solution.py:92
  286.6 8.8 %collective-permute-start.28 = (bf16[32,1792]{1,0:T(8,128)(2,1)S(1)}, bf16[32,1792]{1,0:T(8,128)(2,1)S(1)}, u32[]{:S(2)}, u32[]{:S(2)}) collective-permute-start(bf16[32,1792]{1,0:T(8,128)(2,1)S(1)} %slice.241), channel_id=1, source_target_pairs={{0,16},{1,17},{2,18},{3,19},{4,20},{5,21},{6,22},{7,23},{8,24},{9,... | collective-permute-start | bytes 344072 | tf_op jit(solution)/shard_map/ppermute | solution.py:92
  293.2 15.9 %collective-permute-start.20 = (bf16[64,5632]{1,0:T(8,128)(2,1)S(1)}, bf16[64,5632]{1,0:T(8,128)(2,1)S(1)}, u32[]{:S(2)}, u32[]{:S(2)}) collective-permute-start(bf16[64,5632]{1,0:T(8,128)(2,1)S(1)} %get-tuple-element.97), channel_id=1, source_target_pairs={{0,8},{1,9},{2,10},{3,11},{4,12},{5,13},{6,14},{7,15},{8,0},{9,1},... | collective-permute-start | bytes 2162696 | tf_op jit(solution)/shard_map/ppermute | solution.py:92
  293.8 15.9 %collective-permute-start.22 = (bf16[64,5632]{1,0:T(8,128)(2,1)S(1)}, bf16[64,5632]{1,0:T(8,128)(2,1)S(1)}, u32[]{:S(2)}, u32[]{:S(2)}) collective-permute-start(bf16[64,5632]{1,0:T(8,128)(2,1)S(1)} %get-tuple-element.96), channel_id=1, source_target_pairs={{0,16},{1,17},{2,18},{3,19},{4,20},{5,21},{6,22},{7,23},{8,24},{9,... | collective-permute-start | bytes 2162696 | tf_op jit(solution)/shard_map/ppermute | solution.py:92
  310.1 8.5 %collective-permute-start.23 = (bf16[32,5632]{1,0:T(8,128)(2,1)S(1)}, bf16[32,5632]{1,0:T(8,128)(2,1)S(1)}, u32[]{:S(2)}, u32[]{:S(2)}) collective-permute-start(bf16[32,5632]{1,0:T(8,128)(2,1)S(1)} %slice.237), channel_id=1, source_target_pairs={{0,8},{1,9},{2,10},{3,11},{4,12},{5,13},{6,14},{7,15},{8,0},{9,1},... | collective-permute-start | bytes 1081352 | tf_op jit(solution)/shard_map/ppermute | solution.py:92
  318.7 9.4 %collective-permute-start.24 = (bf16[32,5632]{1,0:T(8,128)(2,1)S(1)}, bf16[32,5632]{1,0:T(8,128)(2,1)S(1)}, u32[]{:S(2)}, u32[]{:S(2)}) collective-permute-start(bf16[32,5632]{1,0:T(8,128)(2,1)S(1)} %fusion), channel_id=1, source_target_pairs={{0,2},{1,3},{2,0},{3,1},{4,6},{5,7},{6,4},{7,5},{8,10},{9,11},{10,... | collective-permute-start | bytes 1081352 | tf_op jit(solution)/shard_map/ppermute | solution.py:92
  328.3 8.4 %collective-permute-start.25 = (bf16[16,5632]{1,0:T(8,128)(2,1)S(1)}, bf16[16,5632]{1,0:T(8,128)(2,1)S(1)}, u32[]{:S(2)}, u32[]{:S(2)}) collective-permute-start(bf16[16,5632]{1,0:T(8,128)(2,1)S(1)} %slice.239), channel_id=1, source_target_pairs={{0,4},{1,5},{2,6},{3,7},{4,0},{5,1},{6,2},{7,3},{8,12},{9,13},{10,... | collective-permute-start | bytes 540680 | tf_op jit(solution)/shard_map/ppermute | solution.py:92
  331.3 8.9 %collective-permute-start.40 = (f32[8,1792]{1,0:T(8,128)S(1)}, f32[8,1792]{1,0:T(8,128)S(1)}, u32[]{:S(2)}, u32[]{:S(2)}) collective-permute-start(f32[8,1792]{1,0:T(8,128)S(1)} %get-tuple-element.126), channel_id=1, source_target_pairs={{0,8},{1,9},{2,10},{3,11},{4,12},{5,13},{6,14},{7,15},{8,0},{9,1},... | collective-permute-start | bytes 172040 | tf_op jit(solution)/shard_map/ppermute | solution.py:92
  340.1 9.1 %collective-permute-start.41 = (f32[16,1792]{1,0:T(8,128)S(1)}, f32[16,1792]{1,0:T(8,128)S(1)}, u32[]{:S(2)}, u32[]{:S(2)}) collective-permute-start(f32[16,1792]{1,0:T(8,128)S(1)} %pad_maximum_fusion.7), channel_id=1, source_target_pairs={{0,16},{1,17},{2,18},{3,19},{4,20},{5,21},{6,22},{7,23},{8,24},{9,... | collective-permute-start | bytes 344072 | tf_op jit(solution)/shard_map/ppermute | solution.py:92
  346.9 7.7 %collective-permute-start.42 = (f32[8,5632]{1,0:T(8,128)S(1)}, f32[8,5632]{1,0:T(8,128)S(1)}, u32[]{:S(2)}, u32[]{:S(2)}) collective-permute-start(f32[8,5632]{1,0:T(8,128)S(1)} %get-tuple-element.108), channel_id=1, source_target_pairs={{0,16},{1,17},{2,18},{3,19},{4,20},{5,21},{6,22},{7,23},{8,24},{9,... | collective-permute-start | bytes 540680 | tf_op jit(solution)/shard_map/ppermute | solution.py:92
  354.7 9.7 %collective-permute-start.43 = (f32[16,5632]{1,0:T(8,128)S(1)}, f32[16,5632]{1,0:T(8,128)S(1)}, u32[]{:S(2)}, u32[]{:S(2)}) collective-permute-start(f32[16,5632]{1,0:T(8,128)S(1)} %pad_maximum_fusion.2), channel_id=1, source_target_pairs={{0,8},{1,9},{2,10},{3,11},{4,12},{5,13},{6,14},{7,15},{8,0},{9,1},... | collective-permute-start | bytes 1081352 | tf_op jit(solution)/shard_map/ppermute | solution.py:92
  (47 other events, 449.0 us)
